TPU v7x, 32 devices: a whole 2x2x4 slice. The times are simulated.
32 devices in a mesh: groups: 2 (over y), chan: 4 (over z), tm: 2 (over x), band: 2 (over core).
Axes of the slice: x: 2, y: 2, z: 4, core: 2. Of those that a mesh axis runs over, the one named last changes fastest.
Arguments:
- recording: float32 [1024, 2048], P(('groups', 'chan'), 'tm'), parts along dimension 0, may hold values from -460 to 460
- tau_index: int32 [1024], P(('groups', 'chan')), parts along dimension 0, may hold values from 0 to 7
- pair_offset: int32 [4, 4], replicated, may hold values from -1 to 3, as said below
Outputs:
- correlations: float32 [8, 4, 3, 128, 128], P(('groups', 'chan'), None, None, ('tm', 'band')), parts along dimension 0
There are 2 independent parts, one for each index of `groups`. A program takes and returns all parts, laid end to end along the dimension named above; an argument that names none is the same for every part. Nothing has to cross between parts.
Inputs may be any that keep to these rules, and one draw needn't show every extreme that they name: pair_offset[i, q] is an offset of 1 to 3 blocks for q below the row's partner count, and -1 from there on; every row has 1 to 4 partners.
All inputs are finite; a program needn't handle non-finite values.
Results may differ from a plain program's by a relative error of at most 0.006.
Values may be sent and summed in bfloat16 or wider, within the bound.
A program may use at most 64 MiB of HBM per device.

v0:
```python
import math
import jax
import jax.numpy as jnp
from jax import lax
from jax.sharding import PartitionSpec as P

BLK = 128
HALO_CH = 64
HALO_T = 256
LAGS = 3
QMAX = 4


def from_behind(block, axis, distance):
    devices = range(lax.axis_size(axis))
    route = [(i - distance, i) for i in devices if i - distance in devices]
    return lax.ppermute(block, axis, route)


def padded_2(block, sides, width):
    for axis, dim in sides:
        count = lax.axis_size(axis)
        forward = [(i, i + 1) for i in range(count - 1)]
        backward = [(target, source) for source, target in forward]
        low = lax.ppermute(
            lax.slice_in_dim(block, block.shape[dim] - width, None, axis=dim), axis, forward
        )
        high = lax.ppermute(lax.slice_in_dim(block, 0, width, axis=dim), axis, backward)
        block = jnp.concatenate([low, block, high], axis=dim)
    return block


def slide_total(padded, reach, size, axis):
    zero_shape = list(padded.shape)
    zero_shape[axis] = 1
    running = jnp.concatenate(
        [jnp.zeros(zero_shape, jnp.float32), jnp.cumsum(padded, axis=axis)], axis=axis
    )
    upper = lax.slice_in_dim(running, 2 * reach + 1, 2 * reach + 1 + size, axis=axis)
    lower = lax.slice_in_dim(running, 0, size, axis=axis)
    return upper - lower


def spatial_filter(padded, center, counted):
    total = slide_total(padded, HALO_CH, center.shape[0], 0)
    return center - total / counted[:, None]


def amplitude_norm(padded, center):
    total = slide_total(jnp.abs(padded), HALO_T, center.shape[1], 1)
    return center / (total / (2.0 * HALO_T + 1.0) + 1e-06)


def shards(recording, tau_index, pair_offset):
    channels, samples = recording.shape
    chan_count = lax.axis_size("chan")
    time_count = lax.axis_size("tm")
    band_count = lax.axis_size("band")
    chan_pos = lax.axis_index("chan")
    time_pos = lax.axis_index("tm")
    band_pos = lax.axis_index("band")
    all_channels = channels * chan_count
    all_samples = samples * time_count
    kept_bins = all_samples // 4
    first_bin = kept_bins // 4
    band_bins = kept_bins // band_count
    device_bins = band_bins // time_count
    decay = jnp.exp(-1.0 / (2.0 * 2.0 ** (tau_index.astype(jnp.float32) / 2.0)))[:, None]
    rows_global = chan_pos * channels + jnp.arange(channels)
    counted = (
        jnp.minimum(rows_global, HALO_CH) + jnp.minimum(all_channels - 1 - rows_global, HALO_CH) + 1
    ).astype(jnp.float32)
    previous = from_behind(recording[:, samples - 1 :], "tm", 1)
    deconv = recording - decay * jnp.concatenate([previous, recording[:, : samples - 1]], axis=1)
    deconv_wide = padded_2(deconv, (("chan", 0),), HALO_CH)
    filtered = spatial_filter(deconv_wide, deconv, counted)
    filtered_wide = padded_2(filtered, (("tm", 1),), HALO_T)
    normed = amplitude_norm(filtered_wide, filtered)
    time_global = time_pos * samples + jnp.arange(samples)
    sub_rows = math.gcd(device_bins * lax.axis_size("tm"), 128)
    pieces = device_bins * lax.axis_size("tm") // sub_rows

    def one_piece(piece_idx):
        bins_here = first_bin + band_pos * band_bins + piece_idx * sub_rows + jnp.arange(sub_rows)
        turns = bins_here[:, None] * time_global[None, :] % all_samples
        angle = 2.0 * jnp.pi / all_samples * turns.astype(jnp.float32)
        dims = (((1,), (1,)), ((), ()))
        real_part = lax.dot_general(
            jnp.cos(angle),
            normed,
            dims,
            precision=lax.Precision.HIGHEST,
            preferred_element_type=jnp.float32,
        )
        imag_part = -lax.dot_general(
            jnp.sin(angle),
            normed,
            dims,
            precision=lax.Precision.HIGHEST,
            preferred_element_type=jnp.float32,
        )
        return jnp.stack([real_part, imag_part], axis=1)

    stacked = lax.map(one_piece, jnp.arange(pieces))
    spectra = lax.psum_scatter(
        stacked.reshape(device_bins * lax.axis_size("tm"), 2, channels),
        "tm",
        scatter_dimension=0,
        tiled=True,
    )
    local_power = jnp.sum(spectra * spectra, axis=(0, 1))
    power = lax.psum(local_power, ("tm", "band"))
    factor = lax.rsqrt(power / kept_bins + 1e-06)
    white = (spectra * factor[None, None, :]).astype(jnp.bfloat16)
    bins_mine = first_bin + band_pos * band_bins + time_pos * device_bins + jnp.arange(device_bins)
    lagged = jnp.arange(LAGS) - LAGS // 2
    phase = (
        2.0
        * jnp.pi
        / all_samples
        * (bins_mine[:, None] * lagged[None, :] % all_samples).astype(jnp.float32)
    )
    cosine = jnp.cos(phase)[:, :, None]
    sine = jnp.sin(phase)[:, :, None]
    white_f = white.astype(jnp.float32)
    real_shift = white_f[:, 0, None, :] * cosine - white_f[:, 1, None, :] * sine
    imag_shift = white_f[:, 0, None, :] * sine + white_f[:, 1, None, :] * cosine
    shifted = jnp.stack([real_shift, imag_shift], axis=1).astype(jnp.bfloat16)
    own_blocks = channels // BLK
    all_blocks = all_channels // BLK
    my_offsets = lax.dynamic_slice_in_dim(pair_offset, chan_pos * own_blocks, own_blocks, 0)
    left_blocks = [shifted.reshape(2 * device_bins, LAGS * BLK)]
    cc_scale = 1.0 / math.sqrt(kept_bins)
    initial = tuple(
        (jnp.zeros((LAGS * BLK, BLK), jnp.float32) for slot_all in range(own_blocks * QMAX))
    )
    piece = lax.all_gather(white, "chan", axis=2, tiled=True)
    width = piece.shape[2]
    updated = []
    for slot_idx in range(QMAX):
        offset = my_offsets[0, slot_idx]
        partner = (chan_pos * own_blocks + 0 + jnp.maximum(offset, 0)) % all_blocks
        local_col = partner * BLK
        present = (offset >= 0) & (local_col >= 0) & (local_col < width)
        clipped = jnp.clip(local_col, 0, width - BLK)
        right = lax.dynamic_slice_in_dim(piece, clipped, BLK, 2)
        right = right.reshape(2 * device_bins, BLK)

        def compute(previous_value, left=left_blocks[0], right=right):
            product = lax.dot_general(
                left, right, (((0,), (0,)), ((), ())), preferred_element_type=jnp.float32
            )
            return product * cc_scale

        def keep(previous_value):
            return previous_value

        updated.append(lax.cond(present, compute, keep, initial[slot_idx]))
    gathered = tuple(updated)
    stacked_cc = jnp.stack(gathered).reshape(own_blocks, QMAX, LAGS, BLK, BLK)
    return lax.psum_scatter(stacked_cc, ("tm", "band"), scatter_dimension=3, tiled=True)


def solution(mesh):
    return jax.shard_map(
        shards,
        mesh=mesh,
        in_specs=(P(("groups", "chan"), "tm"), P(("groups", "chan")), P()),
        out_specs=P(("groups", "chan"), None, None, ("tm", "band"), None),
        check_vma=False,
    )
```

profile of v0, /device:TPU:0, one launch (start us, length us, event | category | flops | bytes accessed | tf_op | source)
XLA Modules:
  0.0 122.5 jit_solution(3115787574492478725)
XLA Ops:
  6.5 0.9 slice.63
  7.5 4.8 %collective-permute-start = (f32[128,1]{1,0:T(8,128)S(1)}, f32[128,1]{1,0:T(8,128)S(1)}, u32[]{:S(2)}, u32[]{:S(2)}) collective-permute-start(f32[128,1]{1,0:T(8,128)S(1)} %slice.63), channel_id=1, source_target_pairs={{0,2},{1,3},{4,6},{5,7},{8,10},{9,11},{12,14},{13,15},{16,18},{17,... | collective-permute-start | bytes 1544 | tf_op jit(solution)/shard_map/ppermute | solution.py:17
  12.3 0.7 divide_exponential_fusion
  13.0 1.2 collective-permute-done
  14.2 1.4 %fusion.34 = f32[128,1024]{1,0:T(8,128)S(1)} fusion(f32[128,1024]{1,0:T(8,128)} %param.13, f32[128,1023]{1,0:T(8,128)} %bitcast.94, f32[128,1]{1,0:T(8,128)S(1)} %collective-permute-done, f32[128]{0:T(128)S(1)} %divide_exponential_fusion), kind=kLoop, calls=%fused_computation.55 | loop fusion | flops 393216 | bytes 1573376 | tf_op jit(solution)/shard_map/sub | solution.py:74
  15.7 3.5 %collective-permute-start.1 = (f32[64,1024]{1,0:T(8,128)S(1)}, f32[64,1024]{1,0:T(8,128)S(1)}, u32[]{:S(2)}, u32[]{:S(2)}) collective-permute-start(f32[64,1024]{1,0:T(8,128)S(1)} %get-tuple-element.262), channel_id=1, source_target_pairs={{0,4},{4,8},{8,12},{1,5},{5,9},{9,13},{2,6},{6,10},{10,14},{3,7},{... | collective-permute-start | bytes 786440 | tf_op jit(solution)/shard_map/ppermute | solution.py:25
  19.2 1.3 %collective-permute-start.2 = (f32[64,1024]{1,0:T(8,128)S(1)}, f32[64,1024]{1,0:T(8,128)S(1)}, u32[]{:S(2)}, u32[]{:S(2)}) collective-permute-start(f32[64,1024]{1,0:T(8,128)S(1)} %get-tuple-element.263), channel_id=1, source_target_pairs={{4,0},{8,4},{12,8},{5,1},{9,5},{13,9},{6,2},{10,6},{14,10},{7,3},{... | collective-permute-start | bytes 786440 | tf_op jit(solution)/shard_map/ppermute | solution.py:28
  20.5 3.4 %collective-permute-done.1 = f32[64,1024]{1,0:T(8,128)S(1)} collective-permute-done((f32[64,1024]{1,0:T(8,128)S(1)}, f32[64,1024]{1,0:T(8,128)S(1)}, u32[]{:S(2)}, u32[]{:S(2)}) %collective-permute-start.1) | collective-permute-done | bytes 262176 | tf_op jit(solution)/shard_map/ppermute | solution.py:25
  23.9 4.1 %collective-permute-done.2 = f32[64,1024]{1,0:T(8,128)S(1)} collective-permute-done((f32[64,1024]{1,0:T(8,128)S(1)}, f32[64,1024]{1,0:T(8,128)S(1)}, u32[]{:S(2)}, u32[]{:S(2)}) %collective-permute-start.2) | collective-permute-done | bytes 262176 | tf_op jit(solution)/shard_map/ppermute | solution.py:28
  28.1 0.8 fusion.25
  29.0 0.1 broadcast_add_fusion.1
  29.1 0.3 copy.31
  29.4 0.1 fusion.33
  29.6 4.0 %collective-permute-start.3 = (f32[128,256]{1,0:T(8,128)S(1)}, f32[128,256]{1,0:T(8,128)S(1)}, u32[]{:S(2)}, u32[]{:S(2)}) collective-permute-start(f32[128,256]{1,0:T(8,128)S(1)} %get-tuple-element.260), channel_id=1, source_target_pairs={{0,2},{1,3},{4,6},{5,7},{8,10},{9,11},{12,14},{13,15},{16,18},{17,... | collective-permute-start | bytes 393224 | tf_op jit(solution)/shard_map/ppermute | solution.py:25
  33.6 1.3 %collective-permute-start.4 = (f32[128,256]{1,0:T(8,128)S(1)}, f32[128,256]{1,0:T(8,128)S(1)}, u32[]{:S(2)}, u32[]{:S(2)}) collective-permute-start(f32[128,256]{1,0:T(8,128)S(1)} %get-tuple-element.261), channel_id=1, source_target_pairs={{2,0},{3,1},{6,4},{7,5},{10,8},{11,9},{14,12},{15,13},{18,16},{19,... | collective-permute-start | bytes 393224 | tf_op jit(solution)/shard_map/ppermute | solution.py:28
  34.9 1.2 collective-permute-done.3
  36.0 4.4 %collective-permute-done.4 = f32[128,256]{1,0:T(8,128)S(1)} collective-permute-done((f32[128,256]{1,0:T(8,128)S(1)}, f32[128,256]{1,0:T(8,128)S(1)}, u32[]{:S(2)}, u32[]{:S(2)}) %collective-permute-start.4) | collective-permute-done | bytes 131104 | tf_op jit(solution)/shard_map/ppermute | solution.py:28
  40.4 0.1 maximum_abs_fusion
  40.5 0.3 copy.32
  40.8 0.5 fusion.23
  41.4 0.3 copy.34
  41.6 0.3 copy.35
  41.9 0.2 fusion.30
  42.1 13.2 %while.13 = (s32[]{:T(128)}, f32[2,128,2,128]{3,1,0,2:T(8,128)S(1)}, s32[2]{0:T(128)S(1)}, s32[]{:T(128)}, f32[128,1024]{1,0:T(8,128)S(1)}, /*index=5*/s32[]{:T(128)}, s32[]{:T(128)}, s32[1]{0:T(128)}) while((s32[]{:T(128)}, f32[2,128,2,128]{3,1,0,2:T(8,128)S(1)}, s32[2]{0:T(128)S(1)}, s32[]{:T(128)}, f32[128,1024]{1,0:T(8,128)S(1)}, ...), condition=%wide.region_5.6_spmd.clone, body=%wide.region_4.5_spmd.clone.sunk | while | flops 406373504 | bytes 1455749 | solution.py:104
  42.1 0.7 dynamic_slice.42
  43.5 2.6 %convolution_bitcast_fusion.2 = f32[128,1,128]{2,0,1:T(8,128)S(1)} fusion(f32[128,1024]{1,0:T(8,128)S(1)} %get-tuple-element.331, s32[1024]{0:T(1024)S(1)} %iota_add_fusion.6, s32[128]{0:T(128)S(1)} %iota_add_fusion.7), kind=kOutput, calls=%fused_computation.15.clone.1 | convolution fusion | flops 203161600 | bytes 594432 | tf_op jit(solution)/shard_map/while/body/eval_jaxpr/dot_general | solution.py:88
  46.1 2.6 %fusion.64 = f32[128,1,128]{2,0,1:T(8,128)S(1)} fusion(f32[128,1024]{1,0:T(8,128)S(1)} %get-tuple-element.331, s32[1024]{0:T(1024)S(1)} %iota_add_fusion.6, s32[128]{0:T(128)S(1)} %iota_add_fusion.7), kind=kOutput, calls=%fused_computation.14.clone.1 | convolution fusion | flops 203177984 | bytes 594432 | tf_op jit(solution)/shard_map/while/body/eval_jaxpr/dot_general | solution.py:95
  48.7 0.7 dynamic_slice.42
  50.1 2.6 %convolution_bitcast_fusion.2 = f32[128,1,128]{2,0,1:T(8,128)S(1)} fusion(f32[128,1024]{1,0:T(8,128)S(1)} %get-tuple-element.331, s32[1024]{0:T(1024)S(1)} %iota_add_fusion.6, s32[128]{0:T(128)S(1)} %iota_add_fusion.7), kind=kOutput, calls=%fused_computation.15.clone.1 | convolution fusion | flops 203161600 | bytes 594432 | tf_op jit(solution)/shard_map/while/body/eval_jaxpr/dot_general | solution.py:88
  52.7 2.6 %fusion.64 = f32[128,1,128]{2,0,1:T(8,128)S(1)} fusion(f32[128,1024]{1,0:T(8,128)S(1)} %get-tuple-element.331, s32[1024]{0:T(1024)S(1)} %iota_add_fusion.6, s32[128]{0:T(128)S(1)} %iota_add_fusion.7), kind=kOutput, calls=%fused_computation.14.clone.1 | convolution fusion | flops 203177984 | bytes 594432 | tf_op jit(solution)/shard_map/while/body/eval_jaxpr/dot_general | solution.py:95
  55.3 0.7 copy-done.1
  56.1 0.7 fusion.43
  61.9 0.1 fusion.39
  62.0 0.1 copy.38
  62.1 0.1 copy.39
  62.3 4.9 %reduce-scatter.3.cloned.1.call-done = f32[128,2,128]{2,0,1:T(8,128)} async-done(((f32[256,2,128]{2,0,1:T(8,128)}), f32[128,2,128]{2,0,1:T(8,128)}) %reduce-scatter.3.cloned.1.call-update) | async-done | bytes 131088 | tf_op jit(solution)/shard_map/reduce_scatter | solution.py:105
  67.1 1.0 multiply_reduce_fusion
  68.1 5.8 %psum.7 = f32[128]{0:T(128)S(1)} all-reduce(f32[128]{0:T(128)S(1)} %multiply_reduce_fusion), channel_id=1, replica_groups=mesh['groups'=2,'chan'=4,'tm'=2,'band'=2] {'tm','band'}, use_global_device_ids=true, to_apply=%region_8.9 | all-reduce | flops 128 | bytes 1024 | tf_op jit(solution)/shard_map/psum | solution.py:112
  73.9 0.9 fusion.40
  74.8 0.3 subtract_convert_fusion
  75.1 0.2 pad_maximum_fusion.2
  75.4 13.0 %all_gather.3 = bf16[128,2,512]{2,0,1:T(8,128)(2,1)S(1)} all-gather(bf16[128,2,128]{2,0,1:T(8,128)(2,1)S(1)} %get-tuple-element.259), channel_id=1, replica_groups=mesh['groups'=2,'chan'=4,'tm'=2,'band'=2] {'chan'}, dimensions={2}, use_global_device_ids=true | all-gather | bytes 327680 | tf_op jit(solution)/shard_map/all_gather | solution.py:137
  88.4 0.8 conditional.4
  88.4 0.3 copy.40
  88.7 0.1 constant_dynamic-slice_fusion
  88.8 0.2 fusion.2
  89.1 0.1 copy.26
  89.2 0.8 conditional.5
  89.2 0.3 copy.41
  89.5 0.1 constant_dynamic-slice_fusion.1
  89.6 0.2 fusion.3
  89.9 0.1 copy.27
  90.0 0.8 conditional.6
  90.0 0.3 copy.42
  90.3 0.1 constant_dynamic-slice_fusion.2
  90.4 0.2 fusion.4
  90.7 0.1 copy.28
  90.8 0.8 conditional.7
  90.8 0.3 copy.43
  91.1 0.1 constant_dynamic-slice_fusion.3
  91.3 0.2 fusion.5
  91.5 0.1 copy.29
  91.6 1.0 pad_maximum_fusion.1
  92.6 23.1 %reduce-scatter.5.cloned.1.call-done = f32[1,4,3,32,128]{4,3,2,1,0:T(8,128)} async-done(((f32[1,4,3,128,128]{4,3,2,1,0:T(8,128)}), f32[1,4,3,32,128]{4,3,2,1,0:T(8,128)}) %reduce-scatter.5.cloned.1.call-update) | async-done | bytes 196624 | tf_op jit(solution)/shard_map/reduce_scatter | solution.py:161
  (32 shorter events, 0.5 us)
Async XLA Ops:
  6.5 28.3 %copy-start = (s32[4,4]{1,0:T(4,128)S(1)}, s32[4,4]{1,0:T(4,128)}, u32[]{:S(2)}) copy-start(s32[4,4]{1,0:T(4,128)} %param.15) | copy-start | bytes 196
  6.5 60.6 %reduce-scatter.3.cloned.1.call-start = ((), (), s32[]{:S(2)}) async-start(), calls=%async_computation.2 | async-start | bytes 393216 | tf_op jit(solution)/shard_map/reduce_scatter | solution.py:105
  7.5 6.7 %collective-permute-start = (f32[128,1]{1,0:T(8,128)S(1)}, f32[128,1]{1,0:T(8,128)S(1)}, u32[]{:S(2)}, u32[]{:S(2)}) collective-permute-start(f32[128,1]{1,0:T(8,128)S(1)} %slice.63), channel_id=1, source_target_pairs={{0,2},{1,3},{4,6},{5,7},{8,10},{9,11},{12,14},{13,15},{16,18},{17,... | collective-permute-start | bytes 1544 | tf_op jit(solution)/shard_map/ppermute | solution.py:17
  15.7 8.2 %collective-permute-start.1 = (f32[64,1024]{1,0:T(8,128)S(1)}, f32[64,1024]{1,0:T(8,128)S(1)}, u32[]{:S(2)}, u32[]{:S(2)}) collective-permute-start(f32[64,1024]{1,0:T(8,128)S(1)} %get-tuple-element.262), channel_id=1, source_target_pairs={{0,4},{4,8},{8,12},{1,5},{5,9},{9,13},{2,6},{6,10},{10,14},{3,7},{... | collective-permute-start | bytes 786440 | tf_op jit(solution)/shard_map/ppermute | solution.py:25
  19.2 8.8 %collective-permute-start.2 = (f32[64,1024]{1,0:T(8,128)S(1)}, f32[64,1024]{1,0:T(8,128)S(1)}, u32[]{:S(2)}, u32[]{:S(2)}) collective-permute-start(f32[64,1024]{1,0:T(8,128)S(1)} %get-tuple-element.263), channel_id=1, source_target_pairs={{4,0},{8,4},{12,8},{5,1},{9,5},{13,9},{6,2},{10,6},{14,10},{7,3},{... | collective-permute-start | bytes 786440 | tf_op jit(solution)/shard_map/ppermute | solution.py:28
  29.6 6.5 %collective-permute-start.3 = (f32[128,256]{1,0:T(8,128)S(1)}, f32[128,256]{1,0:T(8,128)S(1)}, u32[]{:S(2)}, u32[]{:S(2)}) collective-permute-start(f32[128,256]{1,0:T(8,128)S(1)} %get-tuple-element.260), channel_id=1, source_target_pairs={{0,2},{1,3},{4,6},{5,7},{8,10},{9,11},{12,14},{13,15},{16,18},{17,... | collective-permute-start | bytes 393224 | tf_op jit(solution)/shard_map/ppermute | solution.py:25
  33.6 6.9 %collective-permute-start.4 = (f32[128,256]{1,0:T(8,128)S(1)}, f32[128,256]{1,0:T(8,128)S(1)}, u32[]{:S(2)}, u32[]{:S(2)}) collective-permute-start(f32[128,256]{1,0:T(8,128)S(1)} %get-tuple-element.261), channel_id=1, source_target_pairs={{2,0},{3,1},{6,4},{7,5},{10,8},{11,9},{14,12},{15,13},{18,16},{19,... | collective-permute-start | bytes 393224 | tf_op jit(solution)/shard_map/ppermute | solution.py:28
  55.3 0.7 copy-start.1
  56.0 59.6 %reduce-scatter.5.cloned.1.call-start = ((), (), s32[]{:S(2)}) async-start(), calls=%async_computation.3 | async-start | bytes 983040 | tf_op jit(solution)/shard_map/reduce_scatter | solution.py:161
Sparse Core Ops, SparseCore 0:
  56.1 10.9 reduce-scatter.2
  92.7 22.9 reduce-scatter.4
where the time goes:
time: 123 us
  waiting for transfers between devices  42.2 us (34%)
  between operations  18.9 us (15%)
  blocking collectives  18.8 us (15%)
  starting transfers between devices  14.9 us (12%)
  matrix products  11.1 us (9%)
  other arithmetic  7.65 us (6%)
  local copies, waits for them, and re-layouts  7.28 us (6%)
  loops' own time  1.66 us (1%)
    reduce_scatter x1, waiting for transfers between devices, shards(): lax.psum_scatter(stacked_cc, ('tm', 'band'), scatter_dimension=3, tiled=T...  23.1 us
    all_gather x1, blocking collectives, shards(): piece = lax.all_gather(white, 'chan', axis=2, tiled=True)  13 us
    ppermute x2, waiting for transfers between devices, padded_2(): lax.ppermute(lax.slice_in_dim(block, 0, width, axis=dim), axis, backward)  8.49 us
    ppermute x2, starting transfers between devices, padded_2(): lax.ppermute(lax.slice_in_dim(block, block.shape[dim] - width, None, axis...  7.47 us
    psum x1, blocking collectives, shards(): power = lax.psum(local_power, ('tm', 'band'))  5.75 us
    dot_general x2, matrix products, one_piece(): lax.dot_general(jnp.sin(angle), normed, dims, precision=lax.Precision.HIG...  5.16 us
    dot_general x2, matrix products, one_piece(): lax.dot_general(jnp.cos(angle), normed, dims, precision=lax.Precision.HIG...  5.13 us
    reduce_scatter x1, waiting for transfers between devices, shards(): lax.psum_scatter(stacked.reshape(device_bins * lax.axis_size('tm'), 2, ch...  4.85 us
  transfers between devices with their start and end apart: 7, of which 7 were waited for; matrix products, arithmetic and copies ran while one was open for 1% of the time, Pallas kernels for 0%

commit v1 on v0

--- a/solution.py
+++ b/solution.py
@@ -134,7 +134,15 @@
     initial = tuple(
         (jnp.zeros((LAGS * BLK, BLK), jnp.float32) for slot_all in range(own_blocks * QMAX))
     )
-    piece = lax.all_gather(white, "chan", axis=2, tiled=True)
+    ways, here, lap = (lax.axis_size("chan"), lax.axis_index("chan"), white.shape[2])
+    line, have = (white, 1)
+    while have < ways:
+        line = jnp.concatenate(
+            [line, lax.ppermute(line, "chan", [(d, (d - have) % ways) for d in range(ways)])],
+            axis=2,
+        )
+        have = 2 * have
+    piece = jnp.roll(line, here * lap, axis=2)
     width = piece.shape[2]
     updated = []
     for slot_idx in range(QMAX):

time: 123 us -> 125 us (1.016)
  blocking collectives: 18.8 us -> 5.75 us
  waiting for transfers between devices: 42.2 us -> 50.8 us
  starting transfers between devices: 14.9 us -> 20 us
    all_gather x1 -> x0, blocking collectives: 13 us -> none  [shards(): piece = lax.all_gather(white, 'chan', axis=2, tiled=True)]
    ppermute x0 -> x2, waiting for transfers between devices: none -> 7.68 us  [shards(): lax.ppermute(line, 'chan', [(d, (d - have) % ways) for d in range(ways)])]
    ppermute x0 -> x2, starting transfers between devices: none -> 5.07 us  [shards(): lax.ppermute(line, 'chan', [(d, (d - have) % ways) for d in range(ways)])]
  transfers between devices with their start and end apart: 7 -> 9, of which waited for: 7 -> 9; matrix products, arithmetic and copies ran while one was open for 1% -> 2% of each run, Pallas kernels for 0% -> 0%
where the time goes in v1:
time: 125 us; the launch traced here: 124 us
  waiting for transfers between devices  50.8 us (41%)
  starting transfers between devices  20 us (16%)
  between operations  18.8 us (15%)
  matrix products  11.1 us (9%)
  local copies, waits for them, and re-layouts  8.4 us (7%)
  other arithmetic  7.66 us (6%)
  blocking collectives  5.75 us (5%)
  loops' own time  1.89 us (2%)
    reduce_scatter x1, waiting for transfers between devices, shards(): lax.psum_scatter(stacked_cc, ('tm', 'band'), scatter_dimension=3, tiled=T...  23.9 us
    ppermute x2, waiting for transfers between devices, padded_2(): lax.ppermute(lax.slice_in_dim(block, 0, width, axis=dim), axis, backward)  8.49 us
    ppermute x2, waiting for transfers between devices, shards(): lax.ppermute(line, 'chan', [(d, (d - have) % ways) for d in range(ways)])  7.68 us
    ppermute x2, starting transfers between devices, padded_2(): lax.ppermute(lax.slice_in_dim(block, block.shape[dim] - width, None, axis...  7.47 us
    psum x1, blocking collectives, shards(): power = lax.psum(local_power, ('tm', 'band'))  5.75 us
    dot_general x2, matrix products, one_piece(): lax.dot_general(jnp.sin(angle), normed, dims, precision=lax.Precision.HIG...  5.16 us
    dot_general x2, matrix products, one_piece(): lax.dot_general(jnp.cos(angle), normed, dims, precision=lax.Precision.HIG...  5.14 us
    ppermute x2, starting transfers between devices, shards(): lax.ppermute(line, 'chan', [(d, (d - have) % ways) for d in range(ways)])  5.07 us
  transfers between devices with their start and end apart: 9, of which 9 were waited for; matrix products, arithmetic and copies ran while one was open for 2% of the time, Pallas kernels for 0%

profile of v1, /device:TPU:0, one launch (start us, length us, event | category | flops | bytes accessed | tf_op | source)
XLA Modules:
  0.0 124.4 jit_solution(16460726585812545766)
XLA Ops:
  6.5 0.9 slice.63
  7.5 4.8 %collective-permute-start = (f32[128,1]{1,0:T(8,128)S(1)}, f32[128,1]{1,0:T(8,128)S(1)}, u32[]{:S(2)}, u32[]{:S(2)}) collective-permute-start(f32[128,1]{1,0:T(8,128)S(1)} %slice.63), channel_id=1, source_target_pairs={{0,2},{1,3},{4,6},{5,7},{8,10},{9,11},{12,14},{13,15},{16,18},{17,... | collective-permute-start | bytes 1544 | tf_op jit(solution)/shard_map/ppermute | solution.py:17
  12.3 0.7 divide_exponential_fusion
  13.0 1.2 collective-permute-done
  14.2 1.4 %fusion.34 = f32[128,1024]{1,0:T(8,128)S(1)} fusion(f32[128,1024]{1,0:T(8,128)} %param.13, f32[128,1023]{1,0:T(8,128)} %bitcast.94, f32[128,1]{1,0:T(8,128)S(1)} %collective-permute-done, f32[128]{0:T(128)S(1)} %divide_exponential_fusion), kind=kLoop, calls=%fused_computation.55 | loop fusion | flops 393216 | bytes 1573376 | tf_op jit(solution)/shard_map/sub | solution.py:74
  15.7 3.5 %collective-permute-start.1 = (f32[64,1024]{1,0:T(8,128)S(1)}, f32[64,1024]{1,0:T(8,128)S(1)}, u32[]{:S(2)}, u32[]{:S(2)}) collective-permute-start(f32[64,1024]{1,0:T(8,128)S(1)} %get-tuple-element.322), channel_id=1, source_target_pairs={{0,4},{4,8},{8,12},{1,5},{5,9},{9,13},{2,6},{6,10},{10,14},{3,7},{... | collective-permute-start | bytes 786440 | tf_op jit(solution)/shard_map/ppermute | solution.py:25
  19.2 1.3 %collective-permute-start.2 = (f32[64,1024]{1,0:T(8,128)S(1)}, f32[64,1024]{1,0:T(8,128)S(1)}, u32[]{:S(2)}, u32[]{:S(2)}) collective-permute-start(f32[64,1024]{1,0:T(8,128)S(1)} %get-tuple-element.323), channel_id=1, source_target_pairs={{4,0},{8,4},{12,8},{5,1},{9,5},{13,9},{6,2},{10,6},{14,10},{7,3},{... | collective-permute-start | bytes 786440 | tf_op jit(solution)/shard_map/ppermute | solution.py:28
  20.5 3.4 %collective-permute-done.1 = f32[64,1024]{1,0:T(8,128)S(1)} collective-permute-done((f32[64,1024]{1,0:T(8,128)S(1)}, f32[64,1024]{1,0:T(8,128)S(1)}, u32[]{:S(2)}, u32[]{:S(2)}) %collective-permute-start.1) | collective-permute-done | bytes 262176 | tf_op jit(solution)/shard_map/ppermute | solution.py:25
  23.9 4.1 %collective-permute-done.2 = f32[64,1024]{1,0:T(8,128)S(1)} collective-permute-done((f32[64,1024]{1,0:T(8,128)S(1)}, f32[64,1024]{1,0:T(8,128)S(1)}, u32[]{:S(2)}, u32[]{:S(2)}) %collective-permute-start.2) | collective-permute-done | bytes 262176 | tf_op jit(solution)/shard_map/ppermute | solution.py:28
  28.1 0.8 fusion.25
  29.1 0.3 copy.31
  29.4 0.1 fusion.33
  29.6 4.0 %collective-permute-start.3 = (f32[128,256]{1,0:T(8,128)S(1)}, f32[128,256]{1,0:T(8,128)S(1)}, u32[]{:S(2)}, u32[]{:S(2)}) collective-permute-start(f32[128,256]{1,0:T(8,128)S(1)} %get-tuple-element.320), channel_id=1, source_target_pairs={{0,2},{1,3},{4,6},{5,7},{8,10},{9,11},{12,14},{13,15},{16,18},{17,... | collective-permute-start | bytes 393224 | tf_op jit(solution)/shard_map/ppermute | solution.py:25
  33.6 1.3 %collective-permute-start.4 = (f32[128,256]{1,0:T(8,128)S(1)}, f32[128,256]{1,0:T(8,128)S(1)}, u32[]{:S(2)}, u32[]{:S(2)}) collective-permute-start(f32[128,256]{1,0:T(8,128)S(1)} %get-tuple-element.321), channel_id=1, source_target_pairs={{2,0},{3,1},{6,4},{7,5},{10,8},{11,9},{14,12},{15,13},{18,16},{19,... | collective-permute-start | bytes 393224 | tf_op jit(solution)/shard_map/ppermute | solution.py:28
  34.9 1.2 collective-permute-done.3
  36.0 4.4 %collective-permute-done.4 = f32[128,256]{1,0:T(8,128)S(1)} collective-permute-done((f32[128,256]{1,0:T(8,128)S(1)}, f32[128,256]{1,0:T(8,128)S(1)}, u32[]{:S(2)}, u32[]{:S(2)}) %collective-permute-start.4) | collective-permute-done | bytes 131104 | tf_op jit(solution)/shard_map/ppermute | solution.py:28
  40.5 0.3 copy.32
  40.8 0.5 fusion.23
  41.4 0.3 copy.34
  41.6 0.3 copy.35
  41.9 0.2 fusion.30
  42.1 13.1 %while.13 = (s32[]{:T(128)}, f32[2,128,2,128]{3,1,0,2:T(8,128)S(1)}, s32[2]{0:T(128)S(1)}, s32[]{:T(128)}, f32[128,1024]{1,0:T(8,128)S(1)}, /*index=5*/s32[]{:T(128)}, s32[]{:T(128)}, s32[1]{0:T(128)}) while((s32[]{:T(128)}, f32[2,128,2,128]{3,1,0,2:T(8,128)S(1)}, s32[2]{0:T(128)S(1)}, s32[]{:T(128)}, f32[128,1024]{1,0:T(8,128)S(1)}, ...), condition=%wide.region_5.6_spmd.clone, body=%wide.region_4.5_spmd.clone.sunk | while | flops 406373504 | bytes 1455749 | solution.py:104
  42.1 0.7 dynamic_slice.56
  43.5 2.6 %convolution_bitcast_fusion.2 = f32[128,1,128]{2,0,1:T(8,128)S(1)} fusion(f32[128,1024]{1,0:T(8,128)S(1)} %get-tuple-element.391, s32[1024]{0:T(1024)S(1)} %iota_add_fusion.6, s32[128]{0:T(128)S(1)} %iota_add_fusion.7), kind=kOutput, calls=%fused_computation.15.clone.1 | convolution fusion | flops 203161600 | bytes 594432 | tf_op jit(solution)/shard_map/while/body/eval_jaxpr/dot_general | solution.py:88
  46.1 2.6 %fusion.64 = f32[128,1,128]{2,0,1:T(8,128)S(1)} fusion(f32[128,1024]{1,0:T(8,128)S(1)} %get-tuple-element.391, s32[1024]{0:T(1024)S(1)} %iota_add_fusion.6, s32[128]{0:T(128)S(1)} %iota_add_fusion.7), kind=kOutput, calls=%fused_computation.14.clone.1 | convolution fusion | flops 203177984 | bytes 594432 | tf_op jit(solution)/shard_map/while/body/eval_jaxpr/dot_general | solution.py:95
  48.7 0.7 dynamic_slice.56
  50.1 2.6 %convolution_bitcast_fusion.2 = f32[128,1,128]{2,0,1:T(8,128)S(1)} fusion(f32[128,1024]{1,0:T(8,128)S(1)} %get-tuple-element.391, s32[1024]{0:T(1024)S(1)} %iota_add_fusion.6, s32[128]{0:T(128)S(1)} %iota_add_fusion.7), kind=kOutput, calls=%fused_computation.15.clone.1 | convolution fusion | flops 203161600 | bytes 594432 | tf_op jit(solution)/shard_map/while/body/eval_jaxpr/dot_general | solution.py:88
  52.6 2.6 %fusion.64 = f32[128,1,128]{2,0,1:T(8,128)S(1)} fusion(f32[128,1024]{1,0:T(8,128)S(1)} %get-tuple-element.391, s32[1024]{0:T(1024)S(1)} %iota_add_fusion.6, s32[128]{0:T(128)S(1)} %iota_add_fusion.7), kind=kOutput, calls=%fused_computation.14.clone.1 | convolution fusion | flops 203177984 | bytes 594432 | tf_op jit(solution)/shard_map/while/body/eval_jaxpr/dot_general | solution.py:95
  55.3 0.7 copy-done.1
  56.0 0.7 fusion.43
  61.7 0.1 fusion.39
  61.8 0.1 copy.38
  62.1 5.0 %reduce-scatter.3.cloned.1.call-done = f32[128,2,128]{2,0,1:T(8,128)} async-done(((f32[256,2,128]{2,0,1:T(8,128)}), f32[128,2,128]{2,0,1:T(8,128)}) %reduce-scatter.3.cloned.1.call-update) | async-done | bytes 131088 | tf_op jit(solution)/shard_map/reduce_scatter | solution.py:105
  67.1 1.0 multiply_reduce_fusion
  68.1 5.8 %psum.7 = f32[128]{0:T(128)S(1)} all-reduce(f32[128]{0:T(128)S(1)} %multiply_reduce_fusion), channel_id=1, replica_groups=mesh['groups'=2,'chan'=4,'tm'=2,'band'=2] {'tm','band'}, use_global_device_ids=true, to_apply=%region_8.9 | all-reduce | flops 128 | bytes 1024 | tf_op jit(solution)/shard_map/psum | solution.py:112
  73.8 0.9 fusion.40
  74.8 3.6 %collective-permute-start.5 = (bf16[128,2,128]{2,0,1:T(8,128)(2,1)S(1)}, bf16[128,2,128]{2,0,1:T(8,128)(2,1)S(1)}, u32[]{:S(2)}, u32[]{:S(2)}) collective-permute-start(bf16[128,2,128]{2,0,1:T(8,128)(2,1)S(1)} %get-tuple-element.319), channel_id=1, source_target_pairs={{0,12},{4,0},{8,4},{12,8},{1,13},{5,1},{9,5},{13,9},{2,14},{6,2},{... | collective-permute-start | bytes 196616 | tf_op jit(solution)/shard_map/ppermute | solution.py:141
  78.3 0.3 subtract_convert_fusion
  78.7 0.2 pad_maximum_fusion.2
  78.9 1.4 %collective-permute-done.5 = bf16[128,2,128]{2,0,1:T(8,128)(2,1)S(1)} collective-permute-done((bf16[128,2,128]{2,0,1:T(8,128)(2,1)S(1)}, bf16[128,2,128]{2,0,1:T(8,128)(2,1)S(1)}, u32[]{:S(2)}, u32[]{:S(2)}) %collective-permute-start.5) | collective-permute-done | bytes 65568 | tf_op jit(solution)/shard_map/ppermute | solution.py:141
  80.3 1.5 %collective-permute-start.6 = (bf16[128,2,256]{2,0,1:T(8,128)(2,1)S(1)}, bf16[128,2,256]{2,0,1:T(8,128)(2,1)S(1)}, u32[]{:S(2)}, u32[]{:S(2)}) collective-permute-start(bf16[128,2,256]{2,0,1:T(8,128)(2,1)S(1)} %pad_maximum_fusion.3), channel_id=1, source_target_pairs={{0,8},{4,12},{8,0},{12,4},{1,9},{5,13},{9,1},{13,5},{2,10},{6,14},... | collective-permute-start | bytes 393224 | tf_op jit(solution)/shard_map/ppermute | solution.py:141
  81.8 6.3 %collective-permute-done.6 = bf16[128,2,256]{2,0,1:T(8,128)(2,1)S(1)} collective-permute-done((bf16[128,2,256]{2,0,1:T(8,128)(2,1)S(1)}, bf16[128,2,256]{2,0,1:T(8,128)(2,1)S(1)}, u32[]{:S(2)}, u32[]{:S(2)}) %collective-permute-start.6) | collective-permute-done | bytes 131104 | tf_op jit(solution)/shard_map/ppermute | solution.py:141
  88.3 1.1 conditional.4
  88.3 0.5 copy.40
  88.8 0.1 constant_dynamic-slice_fusion
  89.0 0.2 fusion.2
  89.2 0.1 copy.26
  89.3 1.3 %conditional.5 = (f32[1,1,3,128,128]{4,3,2,1,0:T(8,128)S(1)}) conditional(s32[]{:T(128)} %convert_element_type.56, () %tuple.60, (s32[]{:T(128)}, s32[]{:T(128)}, bf16[128,2,1024]{2,0,1:T(8,128)(2,1)S(1)}, bf16[256,384]{1,0:T(8,128)(2,1)S(1)}) %tuple.110), branch_computations={%region_11.12_spmd, %region_12.13_spmd} | conditional | flops 25214980 | bytes 2031680 | solution.py:166
  89.5 0.5 copy.41
  90.1 0.1 constant_dynamic-slice_fusion.1
  90.3 0.2 fusion.3
  90.5 0.1 copy.27
  90.6 1.1 conditional.6
  90.6 0.5 copy.42
  91.2 0.1 constant_dynamic-slice_fusion.2
  91.3 0.2 fusion.4
  91.6 0.1 copy.28
  91.7 1.1 conditional.7
  91.7 0.5 copy.43
  92.3 0.1 constant_dynamic-slice_fusion.3
  92.4 0.2 fusion.5
  92.6 0.1 copy.29
  92.8 0.9 pad_maximum_fusion.1
  93.7 23.9 %reduce-scatter.5.cloned.1.call-done = f32[1,4,3,32,128]{4,3,2,1,0:T(8,128)} async-done(((f32[1,4,3,128,128]{4,3,2,1,0:T(8,128)}), f32[1,4,3,32,128]{4,3,2,1,0:T(8,128)}) %reduce-scatter.5.cloned.1.call-update) | async-done | bytes 196624 | tf_op jit(solution)/shard_map/reduce_scatter | solution.py:169
  (42 shorter events, 0.9 us)
Async XLA Ops:
  6.5 28.3 %copy-start = (s32[4,4]{1,0:T(4,128)S(1)}, s32[4,4]{1,0:T(4,128)}, u32[]{:S(2)}) copy-start(s32[4,4]{1,0:T(4,128)} %param.15) | copy-start | bytes 196
  6.5 60.6 %reduce-scatter.3.cloned.1.call-start = ((), (), s32[]{:S(2)}) async-start(), calls=%async_computation.2 | async-start | bytes 393216 | tf_op jit(solution)/shard_map/reduce_scatter | solution.py:105
  7.5 6.7 %collective-permute-start = (f32[128,1]{1,0:T(8,128)S(1)}, f32[128,1]{1,0:T(8,128)S(1)}, u32[]{:S(2)}, u32[]{:S(2)}) collective-permute-start(f32[128,1]{1,0:T(8,128)S(1)} %slice.63), channel_id=1, source_target_pairs={{0,2},{1,3},{4,6},{5,7},{8,10},{9,11},{12,14},{13,15},{16,18},{17,... | collective-permute-start | bytes 1544 | tf_op jit(solution)/shard_map/ppermute | solution.py:17
  15.7 8.2 %collective-permute-start.1 = (f32[64,1024]{1,0:T(8,128)S(1)}, f32[64,1024]{1,0:T(8,128)S(1)}, u32[]{:S(2)}, u32[]{:S(2)}) collective-permute-start(f32[64,1024]{1,0:T(8,128)S(1)} %get-tuple-element.322), channel_id=1, source_target_pairs={{0,4},{4,8},{8,12},{1,5},{5,9},{9,13},{2,6},{6,10},{10,14},{3,7},{... | collective-permute-start | bytes 786440 | tf_op jit(solution)/shard_map/ppermute | solution.py:25
  19.2 8.8 %collective-permute-start.2 = (f32[64,1024]{1,0:T(8,128)S(1)}, f32[64,1024]{1,0:T(8,128)S(1)}, u32[]{:S(2)}, u32[]{:S(2)}) collective-permute-start(f32[64,1024]{1,0:T(8,128)S(1)} %get-tuple-element.323), channel_id=1, source_target_pairs={{4,0},{8,4},{12,8},{5,1},{9,5},{13,9},{6,2},{10,6},{14,10},{7,3},{... | collective-permute-start | bytes 786440 | tf_op jit(solution)/shard_map/ppermute | solution.py:28
  29.6 6.5 %collective-permute-start.3 = (f32[128,256]{1,0:T(8,128)S(1)}, f32[128,256]{1,0:T(8,128)S(1)}, u32[]{:S(2)}, u32[]{:S(2)}) collective-permute-start(f32[128,256]{1,0:T(8,128)S(1)} %get-tuple-element.320), channel_id=1, source_target_pairs={{0,2},{1,3},{4,6},{5,7},{8,10},{9,11},{12,14},{13,15},{16,18},{17,... | collective-permute-start | bytes 393224 | tf_op jit(solution)/shard_map/ppermute | solution.py:25
  33.6 6.9 %collective-permute-start.4 = (f32[128,256]{1,0:T(8,128)S(1)}, f32[128,256]{1,0:T(8,128)S(1)}, u32[]{:S(2)}, u32[]{:S(2)}) collective-permute-start(f32[128,256]{1,0:T(8,128)S(1)} %get-tuple-element.321), channel_id=1, source_target_pairs={{2,0},{3,1},{6,4},{7,5},{10,8},{11,9},{14,12},{15,13},{18,16},{19,... | collective-permute-start | bytes 393224 | tf_op jit(solution)/shard_map/ppermute | solution.py:28
  55.3 0.7 copy-start.1
  56.0 61.6 %reduce-scatter.5.cloned.1.call-start = ((), (), s32[]{:S(2)}) async-start(), calls=%async_computation.3 | async-start | bytes 983040 | tf_op jit(solution)/shard_map/reduce_scatter | solution.py:169
  74.8 5.5 %collective-permute-start.5 = (bf16[128,2,128]{2,0,1:T(8,128)(2,1)S(1)}, bf16[128,2,128]{2,0,1:T(8,128)(2,1)S(1)}, u32[]{:S(2)}, u32[]{:S(2)}) collective-permute-start(bf16[128,2,128]{2,0,1:T(8,128)(2,1)S(1)} %get-tuple-element.319), channel_id=1, source_target_pairs={{0,12},{4,0},{8,4},{12,8},{1,13},{5,1},{9,5},{13,9},{2,14},{6,2},{... | collective-permute-start | bytes 196616 | tf_op jit(solution)/shard_map/ppermute | solution.py:141
  80.3 7.9 %collective-permute-start.6 = (bf16[128,2,256]{2,0,1:T(8,128)(2,1)S(1)}, bf16[128,2,256]{2,0,1:T(8,128)(2,1)S(1)}, u32[]{:S(2)}, u32[]{:S(2)}) collective-permute-start(bf16[128,2,256]{2,0,1:T(8,128)(2,1)S(1)} %pad_maximum_fusion.3), channel_id=1, source_target_pairs={{0,8},{4,12},{8,0},{12,4},{1,9},{5,13},{9,1},{13,5},{2,10},{6,14},... | collective-permute-start | bytes 393224 | tf_op jit(solution)/shard_map/ppermute | solution.py:141
Sparse Core Ops, SparseCore 0:
  56.1 10.9 reduce-scatter.2
  93.9 23.7 reduce-scatter.4
